TPU v7x, 32 devices: a whole 2x2x4 slice. The times are simulated.
32 devices in a mesh: dp: 8 (over z, x), block: 4 (over y, core).
Axes of the slice: x: 2, y: 2, z: 4, core: 2. Of those that a mesh axis runs over, the one named last changes fastest.
Arguments:
- inputs: bfloat16 [3072, 2048], P('dp', 'block'), may hold values from -6 to 6
- weight_in: bfloat16 [512, 3, 4096], P('dp', None, 'block'), may hold values from -0.15625 to 0.15625
- weight_out: bfloat16 [1024, 3, 2048], P('dp', None, 'block'), may hold values from -0.109375 to 0.109375
- cotangent: bfloat16 [3072, 2048], P('dp', 'block'), may hold values from -6 to 6
Outputs:
- outputs: bfloat16 [3072, 2048], P('dp', 'block')
- input_grad: bfloat16 [3072, 2048], P('dp', 'block')
- grad_in: float32 [512, 3, 4096], P('dp', None, 'block')
- grad_out: float32 [1024, 3, 2048], P('dp', None, 'block')
All inputs are finite; a program needn't handle non-finite values.
Results may differ from a plain program's by a relative error of at most 0.017.
Values may be sent and summed in bfloat16 or wider, within the bound.
A program may use at most 128 MiB of HBM per device.

v0:
```python
import jax
import jax.numpy as jnp
from jax import lax
from jax.sharding import PartitionSpec as P


def swapped(value, axis, distance):
    mask = 2**distance
    pairs = [(source, source ^ mask) for source in range(lax.axis_size(axis))]
    return lax.ppermute(value, axis, pairs)


def gelu_tanh(value):
    return jax.nn.gelu(value, approximate=True)


def rounded(value):
    return lax.optimization_barrier(value.astype(jnp.bfloat16)).astype(jnp.float32)


def reduce_in(in_stack, pre_grad, shard_rows):

    def term(start, count):
        return jnp.einsum("tkc,th->ckh", in_stack, pre_grad, preferred_element_type=jnp.float32)

    return lax.psum_scatter(
        term(jnp.int32(0), lax.axis_size("dp") * shard_rows).astype(jnp.bfloat16),
        "dp",
        scatter_dimension=0,
        tiled=True,
    ).astype(jnp.float32)


def reduce_out(hid_stack, cotangent, shard_rows):

    def term(start, count):
        return jnp.einsum("tkh,tc->hkc", hid_stack, cotangent, preferred_element_type=jnp.float32)

    return lax.psum_scatter(
        term(jnp.int32(0), lax.axis_size("dp") * shard_rows).astype(jnp.bfloat16),
        "dp",
        scatter_dimension=0,
        tiled=True,
    ).astype(jnp.float32)


def body(inputs, weight_in, weight_out, cotangent):
    levels = lax.axis_size("block").bit_length() - 1
    weight_in_all, weight_out_all = (
        lax.all_gather(weight_in, "dp", axis=0, tiled=True),
        lax.all_gather(weight_out, "dp", axis=0, tiled=True),
    )
    pieces = [inputs]
    for level_bit in range(levels):
        pieces.append(swapped(inputs, "block", level_bit))
    in_stack = jnp.stack(pieces, axis=1)
    pre_act = jnp.einsum("tkc,ckh->th", in_stack, weight_in_all, preferred_element_type=jnp.float32)
    hidden = gelu_tanh(pre_act).astype(jnp.bfloat16)
    hid_pieces = [hidden]
    for level_bit in range(levels):
        hid_pieces.append(swapped(hidden, "block", level_bit))
    hid_stack = jnp.stack(hid_pieces, axis=1)
    outputs = jnp.einsum(
        "tkh,hkc->tc", hid_stack, weight_out_all, preferred_element_type=jnp.float32
    ).astype(jnp.bfloat16)
    back_terms = jnp.einsum(
        "tc,hkc->tkh", cotangent, weight_out_all, preferred_element_type=jnp.float32
    )
    back_round = back_terms.astype(jnp.bfloat16)
    hid_grad = rounded(back_terms[:, 0, :])
    for level_bit in range(levels):
        arrived = swapped(back_round[:, level_bit + 1, :], "block", level_bit)
        hid_grad = hid_grad + arrived.astype(jnp.float32)
    slope = jax.vjp(gelu_tanh, pre_act)[1](hid_grad)[0]
    pre_grad = slope.astype(jnp.bfloat16)
    in_terms = jnp.einsum(
        "th,ckh->tkc", pre_grad, weight_in_all, preferred_element_type=jnp.float32
    )
    in_round = in_terms.astype(jnp.bfloat16)
    in_total = rounded(in_terms[:, 0, :])
    for level_bit in range(levels):
        arrived = swapped(in_round[:, level_bit + 1, :], "block", level_bit)
        in_total = in_total + arrived.astype(jnp.float32)
    input_grad = in_total.astype(jnp.bfloat16)
    grad_in = reduce_in(in_stack, pre_grad, weight_in.shape[0])
    grad_out = reduce_out(hid_stack, cotangent, weight_out.shape[0])
    return (outputs, input_grad, grad_in, grad_out)


def solution(mesh):
    placed = (P("dp", "block"), P("dp", None, "block"), P("dp", None, "block"), P("dp", "block"))
    return jax.shard_map(
        body,
        mesh=mesh,
        in_specs=placed,
        out_specs=(
            P("dp", "block"),
            P("dp", "block"),
            P("dp", None, "block"),
            P("dp", None, "block"),
        ),
        check_vma=False,
    )
```

profile of v0, /device:TPU:8, one launch (start us, length us, event | category | flops | bytes accessed | tf_op | source)
XLA Modules:
  0.0 389.2 jit_solution(14098632398219511824)
XLA Ops:
  7.2 0.7 all-gather.5.cloned.1.call-update
  8.0 0.7 all-gather.3.cloned.1.call-update
  8.7 63.1 %all-gather.5.cloned.1.call-done = bf16[1024,3,512]{2,0,1:T(8,128)(2,1)} async-done(((bf16[128,3,512]{2,0,1:T(8,128)(2,1)}), bf16[1024,3,512]{2,0,1:T(8,128)(2,1)}) %all-gather.5.cloned.1.call-update) | async-done | bytes 3145744 | tf_op jit(solution)/shard_map/all_gather | solution.py:51
  71.9 3.3 convert_bitcast_fusion.2
  75.5 1.5 collective-permute-start.5
  77.2 0.6 collective-permute-start.1
  77.7 1.0 collective-permute-done
  78.7 0.7 copy-done.10
  79.5 24.5 %collective-permute-done.1 = bf16[384,512]{1,0:T(8,128)(2,1)} collective-permute-done((bf16[384,512]{1,0:T(8,128)(2,1)S(1)}, bf16[384,512]{1,0:T(8,128)(2,1)}, u32[]{:S(2)}, u32[]{:S(2)}) %collective-permute-start.1) | collective-permute-done | bytes 393248 | tf_op jit(solution)/shard_map/ppermute | solution.py:10
  104.0 29.2 %all-gather.3.cloned.1.call-done = bf16[512,3,1024]{2,0,1:T(8,128)(2,1)} async-done(((bf16[64,3,1024]{2,0,1:T(8,128)(2,1)}), bf16[512,3,1024]{2,0,1:T(8,128)(2,1)}) %all-gather.3.cloned.1.call-update) | async-done | bytes 3145744 | tf_op jit(solution)/shard_map/all_gather | solution.py:50
  133.2 5.9 %fusion.6 = (bf16[384,1024]{1,0:T(8,128)(2,1)S(1)}, bf16[384,1024]{1,0:T(8,128)(2,1)}) fusion(bf16[384,1024]{1,0:T(8,128)(2,1)} %collective-permute-done.5, bf16[384,1024]{1,0:T(8,128)(2,1)S(1)} %collective-permute-done.4, bf16[384,1024]{1,0:T(8,128)(2,1)S(1)} %get-tuple-element.12, bf16[512,3,1024]{2,0,1:T(8,128)(2,1)} %all-gather.3.cloned.1.call-done, ...), kind=kOutput, calls=%fused_computation.12 | convolution fusion | flops 1219756032 | bytes 8257536 | tf_op jit(solution)/shard_map/tkc,ckh->th/dot_general | solution.py:57
  139.1 0.9 copy-done.13
  140.0 2.8 convert_bitcast_fusion.1
  142.8 5.7 %copy.14 = bf16[512,3,1024]{2,1,0:T(4,128)(2,1)} copy(bf16[512,3,1024]{0,2,1:T(8,128)(2,1)S(1)} %convert_bitcast_fusion.1) | data formatting | bytes 6291456 | tf_op jit(solution)/shard_map/convert_element_type | solution.py:27
  148.6 1.1 copy-done.2
  149.6 1.5 collective-permute-start.3
  151.1 0.8 collective-permute-done.2
  151.9 17.7 %collective-permute-done.3 = bf16[384,1024]{1,0:T(8,128)(2,1)S(1)} collective-permute-done((bf16[384,1024]{1,0:T(8,128)(2,1)S(1)}, bf16[384,1024]{1,0:T(8,128)(2,1)S(1)}, u32[]{:S(2)}, u32[]{:S(2)}) %collective-permute-start.3) | collective-permute-done | bytes 786464 | tf_op jit(solution)/shard_map/ppermute | solution.py:10
  169.6 0.9 copy-done.6
  170.5 3.5 convert_bitcast_fusion
  174.0 1.9 copy-done.1
  175.9 2.6 fusion.10
  178.6 1.5 collective-permute-start.7
  180.2 0.6 dynamic-slice
  181.5 8.7 %collective-permute-done.7 = bf16[384,512]{1,0:T(8,128)(2,1)S(1)} collective-permute-done((bf16[384,512]{1,0:T(8,128)(2,1)S(1)}, bf16[384,512]{1,0:T(8,128)(2,1)S(1)}, u32[]{:S(2)}, u32[]{:S(2)}) %collective-permute-start.7) | collective-permute-done | bytes 393248 | tf_op jit(solution)/shard_map/ppermute | solution.py:10
  190.2 0.9 add_convert_fusion
  191.1 4.0 %fusion.11 = bf16[384,512]{1,0:T(8,128)(2,1)} fusion(bf16[1024,3,512]{2,0,1:T(8,128)(2,1)} %all-gather.5.cloned.1.call-done, bf16[384,1,1024]{2,0,1:T(8,128)(2,1)S(1)} %bitcast.68, bf16[384,1,1024]{2,0,1:T(8,128)(2,1)S(1)} %bitcast.66, bf16[384,1,1024]{2,0,1:T(8,128)(2,1)S(1)} %bitcast.64), kind=kOutput, calls=%fused_computation.21 | convolution fusion | flops 1210515456 | bytes 5898240 | tf_op jit(solution)/shard_map/tkh,hkc->tc/dot_general | solution.py:63
  195.1 106.8 %all-reduce.3.cloned.1.call-done = bf16[512,3,1024]{2,1,0:T(4,128)(2,1)} async-done(((bf16[512,3,1024]{2,1,0:T(4,128)(2,1)}), bf16[512,3,1024]{2,1,0:T(4,128)(2,1)}) %all-reduce.3.cloned.1.call-update) | async-done | bytes 3145744
  301.9 1.2 dynamic-slice_convert_fusion
  303.1 1.3 copy.16
  304.4 76.3 %reduce-scatter.2.cloned.1.call-done = bf16[128,3,512]{2,0,1:T(8,128)(2,1)} async-done(((bf16[1024,3,512]{2,0,1:T(8,128)(2,1)}), bf16[128,3,512]{2,0,1:T(8,128)(2,1)}) %reduce-scatter.2.cloned.1.call-update) | async-done | bytes 393232 | tf_op jit(solution)/shard_map/reduce_scatter | solution.py:39
  380.7 2.0 convert_element_type.75
  (38 shorter events, 0.8 us)
Async XLA Ops:
  7.2 64.7 %copy-start = (bf16[384,512]{1,0:T(8,128)(2,1)S(1)}, bf16[384,512]{1,0:T(8,128)(2,1)}, u32[]{:S(2)}) copy-start(bf16[384,512]{1,0:T(8,128)(2,1)} %param.7) | copy-start | bytes 1179652
  7.2 64.7 %all-gather.5.cloned.1.call-start = ((), (), s32[]{:S(2)}) async-start(), calls=%async_computation.2 | async-start | bytes 3538944 | tf_op jit(solution)/shard_map/all_gather | solution.py:51
  7.9 125.3 %all-gather.3.cloned.1.call-start = ((), (), s32[]{:S(2)}) async-start(), calls=%async_computation.1 | async-start | bytes 3538944 | tf_op jit(solution)/shard_map/all_gather | solution.py:50
  8.7 293.2 %all-reduce.3.cloned.1.call-start = ((), (), s32[]{:S(2)}) async-start(), calls=%async_computation.4 | async-start | bytes 8388608
  75.2 1.8 copy-start.8
  75.4 57.8 %collective-permute-start.4 = (bf16[384,1024]{1,0:T(8,128)(2,1)S(1)}, bf16[384,1024]{1,0:T(8,128)(2,1)S(1)}, u32[]{:S(2)}, u32[]{:S(2)}) collective-permute-start(bf16[384,1024]{1,0:T(8,128)(2,1)S(1)} %get-tuple-element.14), channel_id=1, source_target_pairs={{0,1},{1,0},{2,3},{3,2},{4,5},{5,4},{6,7},{7,6},{8,9},{9,8},{10,11... | collective-permute-start | bytes 2359304 | tf_op jit(solution)/shard_map/ppermute | solution.py:10
  75.5 57.7 %collective-permute-start.5 = (bf16[384,1024]{1,0:T(8,128)(2,1)S(1)}, bf16[384,1024]{1,0:T(8,128)(2,1)}, u32[]{:S(2)}, u32[]{:S(2)}) collective-permute-start(bf16[384,1024]{1,0:T(8,128)(2,1)S(1)} %get-tuple-element.13), channel_id=1, source_target_pairs={{0,2},{1,3},{2,0},{3,1},{4,6},{5,7},{6,4},{7,5},{8,10},{9,11},{10,... | collective-permute-start | bytes 2359304 | tf_op jit(solution)/shard_map/ppermute | solution.py:10
  77.0 1.7 collective-permute-start
  77.2 26.8 %collective-permute-start.1 = (bf16[384,512]{1,0:T(8,128)(2,1)S(1)}, bf16[384,512]{1,0:T(8,128)(2,1)}, u32[]{:S(2)}, u32[]{:S(2)}) collective-permute-start(bf16[384,512]{1,0:T(8,128)(2,1)S(1)} %copy-done.8), channel_id=1, source_target_pairs={{0,2},{1,3},{2,0},{3,1},{4,6},{5,7},{6,4},{7,5},{8,10},{9,11},{10,... | collective-permute-start | bytes 1179656 | tf_op jit(solution)/shard_map/ppermute | solution.py:10
  78.7 0.7 copy-start.10
  133.2 6.8 %copy-start.9 = (bf16[384,512]{1,0:T(8,128)(2,1)S(1)}, bf16[384,512]{1,0:T(8,128)(2,1)}, u32[]{:S(2)}) copy-start(bf16[384,512]{1,0:T(8,128)(2,1)} %param.4) | copy-start | bytes 1179652
  133.2 6.8 %copy-start.11 = (bf16[384,512]{1,0:T(8,128)(2,1)S(1)}, bf16[384,512]{1,0:T(8,128)(2,1)}, u32[]{:S(2)}) copy-start(bf16[384,512]{1,0:T(8,128)(2,1)} %copy-done.10) | copy-start | bytes 1179652
  139.1 0.9 copy-start.13
  148.5 1.1 copy-start.2
  148.5 232.2 %reduce-scatter.2.cloned.1.call-start = ((), (), s32[]{:S(2)}) async-start(), calls=%async_computation.3 | async-start | bytes 3538944 | tf_op jit(solution)/shard_map/reduce_scatter | solution.py:39
  149.6 2.3 collective-permute-start.2
  149.6 20.0 %collective-permute-start.3 = (bf16[384,1024]{1,0:T(8,128)(2,1)S(1)}, bf16[384,1024]{1,0:T(8,128)(2,1)S(1)}, u32[]{:S(2)}, u32[]{:S(2)}) collective-permute-start(bf16[384,1024]{1,0:T(8,128)(2,1)S(1)} %copy-done.2), channel_id=1, source_target_pairs={{0,2},{1,3},{2,0},{3,1},{4,6},{5,7},{6,4},{7,5},{8,10},{9,11},{10,... | collective-permute-start | bytes 2359304 | tf_op jit(solution)/shard_map/ppermute | solution.py:10
  151.9 17.7 %copy-start.4 = (bf16[384,1024]{1,0:T(8,128)(2,1)}, bf16[384,1024]{1,0:T(8,128)(2,1)S(1)}, u32[]{:S(2)}) copy-start(bf16[384,1024]{1,0:T(8,128)(2,1)S(1)} %collective-permute-done.2) | copy-start | bytes 2359300
  169.6 0.9 copy-start.6
  174.0 1.9 copy-start.1
  178.4 1.7 copy-start.12
  178.5 12.6 %copy-start.3 = (bf16[384,1024]{1,0:T(8,128)(2,1)S(1)}, bf16[384,1024]{1,0:T(8,128)(2,1)}, u32[]{:S(2)}) copy-start(bf16[384,1024]{1,0:T(8,128)(2,1)} %get-tuple-element.16) | copy-start | bytes 2359300
  178.6 2.9 collective-permute-start.6
  178.6 11.5 %collective-permute-start.7 = (bf16[384,512]{1,0:T(8,128)(2,1)S(1)}, bf16[384,512]{1,0:T(8,128)(2,1)S(1)}, u32[]{:S(2)}, u32[]{:S(2)}) collective-permute-start(bf16[384,512]{1,0:T(8,128)(2,1)S(1)} %get-tuple-element.18), channel_id=1, source_target_pairs={{0,2},{1,3},{2,0},{3,1},{4,6},{5,7},{6,4},{7,5},{8,10},{9,11},{10,... | collective-permute-start | bytes 1179656 | tf_op jit(solution)/shard_map/ppermute | solution.py:10
  181.4 9.6 %copy-start.5 = (bf16[384,1024]{1,0:T(8,128)(2,1)S(1)}, bf16[384,1024]{1,0:T(8,128)(2,1)}, u32[]{:S(2)}) copy-start(bf16[384,1024]{1,0:T(8,128)(2,1)} %copy-done.4) | copy-start | bytes 2359300
  181.4 9.6 %copy-start.7 = (bf16[384,1024]{1,0:T(8,128)(2,1)S(1)}, bf16[384,1024]{1,0:T(8,128)(2,1)}, u32[]{:S(2)}) copy-start(bf16[384,1024]{1,0:T(8,128)(2,1)} %copy-done.6) | copy-start | bytes 2359300
Sparse Core Ops, SparseCore 0:
  10.2 61.6 all-gather.4
  74.0 59.1 all-gather.2
  148.7 153.1 all-reduce.2
  305.3 75.2 reduce-scatter.1
where the time goes:
time: 392 us; the launch traced here: 389 us
  waiting for transfers between devices  330 us (84%)
  matrix products  22.1 us (6%)
  between operations  14.6 us (4%)
  local copies, waits for them, and re-layouts  13.3 us (3%)
  starting transfers between devices  5.58 us (1%)
  other arithmetic  4.03 us (1%)
    unnamed x5, waiting for transfers between devices  108 us
    reduce_scatter x1, waiting for transfers between devices, reduce_out(): lax.psum_scatter(term(jnp.int32(0), lax.axis_size('dp') * shard_rows).ast...  76.3 us
    all_gather x1, waiting for transfers between devices, body(): lax.all_gather(weight_out, 'dp', axis=0, tiled=True)  63.1 us
    ppermute x8, waiting for transfers between devices, swapped(): return lax.ppermute(value, axis, pairs)  52.7 us
    all_gather x1, waiting for transfers between devices, body(): lax.all_gather(weight_in, 'dp', axis=0, tiled=True)  29.2 us
  transfers between devices with their start and end apart: 12, of which 9 were waited for; matrix products, arithmetic and copies ran while one was open for 5% of the time, Pallas kernels for 0%

commit v1 on v0

v1 whole, which is shorter than its diff:
```python
import functools

import jax
import jax.numpy as jnp
from jax import lax
from jax.experimental import pallas as pl
from jax.experimental.pallas import tpu as pltpu
from jax.sharding import PartitionSpec as P

MESH = pl.DeviceIdType.MESH
F32, BF16 = jnp.float32, jnp.bfloat16
GELU_C, GELU_A = 0.7978845608028654, 0.044715


def dot(a, b, ca, cb):
    return lax.dot_general(a, b, (((ca,), (cb,)), ((), ())), preferred_element_type=F32)


def tiles(total, size, step):
    size = min(size, total)

    def one(i, carry):
        step(pl.ds(pl.multiple_of(i * size, size), size))
        return carry

    lax.fori_loop(0, total // size, one, 0)


def kernel(
    Z, X, L, x_ref, ct_ref, wi_ref, wo_ref, out_ref, ig_ref, gi_ref, go_ref,
    wo, wi, xg, cg, ht_own, ht_send, ht_recv, hg, pg, gi_send, gi_recv, go_send, go_recv,
    ig_send, ig_recv, o_send, o_recv,
    wo_s, wo_r, wi_s, wi_r, x_s, x_r, ct_s, ct_r, ht_s, ht_r, hg_s, hg_r, gi_s, gi_r, go_s, go_r,
    ig_s, ig_r, o_s, o_r,
):
    dp, b = lax.axis_index("dp"), lax.axis_index("block")
    z, x = dp // X, dp % X
    T, C = x_ref.shape
    R1, R2 = wi_ref.shape[2], wo_ref.shape[1]
    TX, HX = X * T, Z * R2

    def flip(k):
        if k == 0:
            return b
        d = 2 ** (k - 1)
        return b + d - 2 * d * ((b // d) % 2)

    def zat(o):
        return (z + o) % Z

    def xat(o):
        return (x + o) % X

    grid = [(oz, ox) for oz in range(Z) for ox in range(X) if oz or ox]
    near = [(ox, k) for k in reversed(range(L)) for ox in range(X) if ox or k]
    rows_t = pl.ds(pl.multiple_of(x * T, T), T)
    rows_1 = pl.ds(pl.multiple_of(dp * R1, R1), R1)
    rows_2 = pl.ds(pl.multiple_of(z * R2, R2), R2)

    sent = []

    def send(src, dst, ssem, rsem, zd, xd, bd):
        c = pltpu.make_async_remote_copy(
            src_ref=src, dst_ref=dst, send_sem=ssem, recv_sem=rsem,
            device_id=(zd * X + xd, bd), device_id_type=MESH,
        )
        c.start()
        sent.append(c)
        return c

    barrier = pltpu.get_barrier_semaphore()
    for oz, ox in grid:
        pl.semaphore_signal(barrier, inc=1, device_id=(zat(oz) * X + xat(ox), b), device_id_type=MESH)
    for ox, k in near:
        if k:
            pl.semaphore_signal(barrier, inc=1, device_id=(z * X + xat(ox), flip(k)), device_id_type=MESH)
    wo[:, rows_2, :] = wo_ref[...]
    wi[:, rows_1, :] = wi_ref[x]
    xg[0, rows_t, :] = x_ref[...]
    cg[rows_t, :] = ct_ref[...]
    pl.semaphore_wait(barrier, len(grid) + X * (L - 1))

    wo_c = [
        send(wo_ref, wo.at[:, rows_2, :], wo_s.at[o], wo_r.at[o], zat(o), x, b)
        for o in range(1, Z)
    ]
    ct_c = [
        send(ct_ref, cg.at[rows_t, :], ct_s.at[o], ct_r.at[o], z, xat(o), b) for o in range(1, X)
    ]
    x_c = [
        send(x_ref, xg.at[k, rows_t, :], x_s.at[ox, k], x_r.at[ox, k], z, xat(ox), flip(k))
        for ox, k in near
    ]
    wi_c = [
        send(wi_ref.at[xat(ox)], wi.at[:, rows_1, :], wi_s.at[oz, ox], wi_r.at[oz, ox], zat(oz), xat(ox), b)
        for oz, ox in grid
    ]

    for c in ct_c + wo_c:
        c.wait_recv()
    ht_c = []
    for k in reversed(range(L)):

        def back(rows, k=k):
            term = dot(cg[rows, :], wo[k], 1, 1).astype(BF16)
            if k:
                ht_send[k - 1, rows, :] = term
            else:
                ht_own[rows, :] = term

        tiles(TX, 256, back)
        if k:
            ht_c.append(
                send(ht_send.at[k - 1], ht_recv.at[k - 1], ht_s.at[k], ht_r.at[k], z, x, flip(k))
            )

    for c in x_c + wi_c + ht_c:
        c.wait_recv()

    def middle(rows):
        v = dot(xg[0, rows, :], wi[0], 1, 0)
        for k in range(1, L):
            v = v + dot(xg[k, rows, :], wi[k], 1, 0)
        g = ht_own[rows, :].astype(F32)
        for k in range(1, L):
            g = g + ht_recv[k - 1, rows, :].astype(F32)
        v2 = v * v
        t = jnp.tanh(GELU_C * v * (1.0 + GELU_A * v2))
        half = 0.5 + 0.5 * t
        hg[0, rows, :] = (v * half).astype(BF16)
        slope = half + 0.5 * v * (1.0 - t * t) * (GELU_C * (1.0 + 3.0 * GELU_A * v2))
        pg[rows, :] = (g * slope).astype(BF16)

    tiles(TX, 128, middle)
    hg_c = [
        send(hg.at[0], hg.at[k], hg_s.at[k], hg_r.at[k], z, x, flip(k))
        for k in reversed(range(1, L))
    ]

    for k in range(L):

        def grad_in(rows, k=k):
            gi_send[k, rows, :] = dot(xg[k, :, rows], pg[...], 0, 0).astype(BF16)

        tiles(C, 256, grad_in)
    gi_c = [
        send(
            gi_send.at[:, pl.ds(pl.multiple_of((zat(oz) * X + xat(ox)) * R1, R1), R1), :],
            gi_recv.at[oz, ox], gi_s.at[oz, ox], gi_r.at[oz, ox], zat(oz), xat(ox), b,
        )
        for oz, ox in grid
    ]

    ig_c = []
    for k in reversed(range(L)):

        def grad_x(rows, k=k):
            ig_send[k, rows, :] = dot(pg[rows, :], wi[k], 1, 1).astype(BF16)

        tiles(TX, 256, grad_x)
        for ox in range(X):
            if ox or k:
                ig_c.append(
                    send(
                        ig_send.at[k, pl.ds(pl.multiple_of(xat(ox) * T, T), T), :],
                        ig_recv.at[k, ox], ig_s.at[ox, k], ig_r.at[ox, k], z, xat(ox), flip(k),
                    )
                )

    for k in range(L):
        if k:
            hg_c[L - 1 - k].wait_recv()

        def grad_out(rows, k=k):
            go_send[k, rows, :] = dot(hg[k, :, rows], cg[...], 0, 0).astype(BF16)

        tiles(HX, 256, grad_out)
    go_c = [
        send(
            go_send.at[:, pl.ds(pl.multiple_of(zat(o) * R2, R2), R2), :],
            go_recv.at[o], go_s.at[o], go_r.at[o], zat(o), x, b,
        )
        for o in range(1, Z)
    ]

    def forward(rows):
        total = dot(hg[0, rows, :], wo[0], 1, 0)
        for k in range(1, L):
            total = total + dot(hg[k, rows, :], wo[k], 1, 0)
        o_send[rows, :] = total.astype(BF16)

    tiles(TX, 256, forward)
    o_c = [
        send(
            o_send.at[pl.ds(pl.multiple_of(xat(o) * T, T), T), :],
            o_recv.at[o], o_s.at[o], o_r.at[o], z, xat(o), b,
        )
        for o in range(1, X)
    ]

    for c in ig_c:
        c.wait_recv()
    total = ig_send[0, rows_t, :].astype(F32)
    for ox, k in near:
        total = total + ig_recv[k, ox].astype(F32)
    ig_ref[...] = total.astype(BF16)
    for c in o_c:
        c.wait_recv()
    total = o_send[rows_t, :].astype(F32)
    for o in range(1, X):
        total = total + o_recv[o].astype(F32)
    out_ref[...] = total.astype(BF16)
    for c in gi_c:
        c.wait_recv()
    for k in range(L):
        for ox in range(X):
            if ox:
                total = gi_recv[0, ox, k].astype(F32)
            else:
                total = gi_send[k, rows_1, :].astype(F32)
            for oz in range(1, Z):
                total = total + gi_recv[oz, ox, k].astype(F32)
            gi_ref[(x + X - ox) % X, k] = total
    for c in go_c:
        c.wait_recv()
    for k in range(L):
        total = go_send[k, rows_2, :].astype(F32)
        for o in range(1, Z):
            total = total + go_recv[o, k].astype(F32)
        go_ref[k] = total
    for c in sent:
        c.wait_send()


def body(Z, X, inputs, weight_in, weight_out, cotangent):
    T, C = inputs.shape
    R1, L, panel = weight_in.shape
    R2 = weight_out.shape[0]
    TX, HX = X * T, Z * R2
    wi = weight_in.reshape(R1, L, Z, X, R2).transpose(3, 1, 0, 2, 4).reshape(X, L, R1, HX)
    wo = weight_out.transpose(1, 0, 2)
    vmem = pl.BlockSpec(memory_space=pltpu.VMEM)

    def buf(*shape):
        return pltpu.VMEM(shape, BF16)

    def sems(*shape):
        return [pltpu.SemaphoreType.DMA(shape)] * 2

    flops = 12 * TX * HX * C * L
    out, ig, gi, go = pl.pallas_call(
        functools.partial(kernel, Z, X, L),
        out_shape=(
            jax.ShapeDtypeStruct((T, C), BF16),
            jax.ShapeDtypeStruct((T, C), BF16),
            jax.ShapeDtypeStruct((X, L, R1, HX), F32),
            jax.ShapeDtypeStruct((L, R2, C), F32),
        ),
        in_specs=[vmem] * 4,
        out_specs=(vmem,) * 4,
        scratch_shapes=[
            buf(L, HX, C), buf(L, C, HX), buf(L, TX, C), buf(TX, C),
            buf(TX, HX), buf(L - 1, TX, HX), buf(L - 1, TX, HX),
            buf(L, TX, HX), buf(TX, HX),
            buf(L, C, HX), buf(Z, X, L, R1, HX), buf(L, HX, C), buf(Z, L, R2, C),
            buf(L, TX, C), buf(L, X, T, C), buf(TX, C), buf(X, T, C),
            *sems(Z), *sems(Z, X), *sems(X, L), *sems(X), *sems(L), *sems(L),
            *sems(Z, X), *sems(Z), *sems(X, L), *sems(X),
        ],
        compiler_params=pltpu.CompilerParams(
            collective_id=0, has_side_effects=True, vmem_limit_bytes=56 * 2**20
        ),
        cost_estimate=pl.CostEstimate(flops=flops, bytes_accessed=8 * 2**20, transcendentals=TX * HX),
    )(inputs, cotangent, wi, wo)
    grad_in = gi.reshape(X, L, R1, Z, R2).transpose(2, 1, 3, 0, 4).reshape(R1, L, panel)
    return out, ig, grad_in, go.transpose(1, 0, 2)


def solution(mesh):
    n = mesh.shape["dp"]
    Z = 4 if n % 4 == 0 else n
    placed = (P("dp", "block"), P("dp", None, "block"), P("dp", None, "block"), P("dp", "block"))
    return jax.shard_map(
        functools.partial(body, Z, n // Z),
        mesh=mesh,
        in_specs=placed,
        out_specs=(
            P("dp", "block"),
            P("dp", "block"),
            P("dp", None, "block"),
            P("dp", None, "block"),
        ),
        check_vma=False,
    )
```

time: 392 us -> 158 us (0.40)
  waiting for transfers between devices: 330 us -> 0 us
  Pallas kernels: 0 us -> 148 us
  matrix products: 22.1 us -> 0 us
  between operations: 14.6 us -> 0.68 us
  starting transfers between devices: 5.58 us -> 0 us
  local copies, waits for them, and re-layouts: 13.3 us -> 8.15 us
  other arithmetic: 4.03 us -> 0 us
    pallas_call x0 -> x1, Pallas kernels: none -> 148 us  [body(): pl.pallas_call(functools.partial(kernel, Z, X, L), out_shape=(jax.ShapeDt...]
    unnamed x5 -> x0, waiting for transfers between devices: 108 us -> none
    all_gather x2 -> x0, waiting for transfers between devices: 92.4 us -> none  [the longest x1 63.1 us: body(): lax.all_gather(weight_out, 'dp', axis=0, tiled=True)]
    reduce_scatter x1 -> x0, waiting for transfers between devices: 76.3 us -> none  [reduce_out(): lax.psum_scatter(term(jnp.int32(0), lax.axis_size('dp') * shard_rows).ast...]
    ppermute x8 -> x0, waiting for transfers between devices: 52.7 us -> none  [swapped(): return lax.ppermute(value, axis, pairs)]
    dot_general x6 -> x0, matrix products: 22.1 us -> none  [the longest x1 5.9 us: body(): jnp.einsum('tkc,ckh->th', in_stack, weight_in_all, preferred_element_type...]
    convert_element_type x3 -> x0, local copies, waits for them, and re-layouts: 5.95 us -> none  [the longest x1 5.66 us: reduce_in(): term(jnp.int32(0), lax.axis_size('dp') * shard_rows).astype(jnp.bfloat16)]
    ppermute x8 -> x0, starting transfers between devices: 5.43 us -> none  [swapped(): return lax.ppermute(value, axis, pairs)]
  transfers between devices with their start and end apart: 12 -> 0, of which waited for: 9 -> 0; matrix products, arithmetic and copies ran while one was open for 5% -> 0% of each run, Pallas kernels for 0% -> 0%
where the time goes in v1:
time: 158 us; the launch traced here: 157 us
  Pallas kernels  148 us (94%)
  local copies, waits for them, and re-layouts  8.15 us (5%)
    pallas_call x1, Pallas kernels, body(): pl.pallas_call(functools.partial(kernel, Z, X, L), out_shape=(jax.ShapeDt...  148 us

profile of v1, /device:TPU:8, one launch (start us, length us, event | category | flops | bytes accessed | tf_op | source)
XLA Modules:
  0.0 156.9 jit_solution(7054734336109793563)
XLA Ops:
  0.6 1.3 reshape.20
  1.9 0.1 copy.11
  2.0 0.9 reshape.21.wi_ref
  2.9 148.1 %shard_map.75 = (bf16[384,512]{1,0:T(8,128)(2,1)}, bf16[384,512]{1,0:T(8,128)(2,1)}, f32[2,3,64,512]{3,2,1,0:T(8,128)}, f32[3,128,512]{2,1,0:T(8,128)}) custom-call(bf16[384,512]{1,0:T(8,128)(2,1)} %x_ref.1, bf16[384,512]{1,0:T(8,128)(2,1)} %ct_ref.1, bf16[2,3,64,512]{3,2,1,0:T(8,128)(2,1)} %reshape.21.wi_ref, bf16[3,128,512]{2,1,0:T(8,128)(2,1)} %bitcast.15), custom_call_target="tpu_custom_call" | custom-call | flops 7247757312 | bytes 8388608 | tf_op jit(solution)/shard_map/pallas_call | solution.py:251
  151.0 1.4 reshape.22
  152.4 0.6 copy.9
  153.0 0.0 copy-start.2
  153.0 0.0 copy-start.1
  153.0 1.5 reshape.23
  154.6 0.0 copy-done.2
  154.6 0.0 copy-start
  154.6 0.7 copy.15
  155.3 0.0 copy-done.1
  155.3 0.7 copy.16
  156.1 0.0 copy-done
  156.1 0.9 copy.17
Async XLA Ops:
  153.0 1.5 copy-start.2
  153.0 2.3 %copy-start.1 = (bf16[384,512]{1,0:T(8,128)(2,1)S(1)}, bf16[384,512]{1,0:T(8,128)(2,1)}, u32[]{:S(2)}) copy-start(bf16[384,512]{1,0:T(8,128)(2,1)} %get-tuple-element.17) | copy-start | bytes 1179652
  154.6 1.5 copy-start

commit v2 on v0

v2 whole, which is shorter than its diff:
```python
import functools

import jax
import jax.numpy as jnp
from jax import lax
from jax.experimental import pallas as pl
from jax.experimental.pallas import tpu as pltpu
from jax.sharding import PartitionSpec as P

MESH = pl.DeviceIdType.MESH
F32, BF16 = jnp.float32, jnp.bfloat16
GELU_C, GELU_A = 0.7978845608028654, 0.044715


def dot(a, b, ca, cb):
    return lax.dot_general(a, b, (((ca,), (cb,)), ((), ())), preferred_element_type=F32)


def tiles(total, size, step):
    size = min(size, total)

    def one(i, carry):
        step(pl.ds(pl.multiple_of(i * size, size), size))
        return carry

    lax.fori_loop(0, total // size, one, 0)


def kernel(
    Z, X, L, x_ref, ct_ref, wi_ref, wo_ref, out_ref, ig_ref, gi_ref, go_ref,
    wo, wi, xg, cg, pa, ht_own, ht_send, ht_recv, hg, pg, gi_part, gi_up, gi_dn, gx_send, gx_recv, acc,
    go_part, go_up, go_dn, ig_send, ig_recv, ig_sum, ig_x, o_send, o_recv,
    wo_us, wo_ur, wo_ds, wo_dr, wi_us, wi_ur, wi_ds, wi_dr, gi_us, gi_ur, gi_ds, gi_dr, go_us, go_ur, go_ds, go_dr,
    wx_s, wx_r, gx_s, gx_r, xx_s, xx_r, x_s, x_r, ct_s, ct_r, ht_s, ht_r, hg_s, hg_r, ig_s, ig_r, igx_s, igx_r, o_s, o_r,
):
    dp, b = lax.axis_index("dp"), lax.axis_index("block")
    z, x = dp // X, dp % X
    T, C = x_ref.shape
    R1, R2 = wi_ref.shape[2], wo_ref.shape[1]
    TX, HX, RX = X * T, Z * R2, X * R1

    def flip(k):
        d = 2 ** (k - 1)
        return b + d - 2 * d * ((b // d) % 2)

    def xat(o):
        return (x + o) % X

    def rows(index, size):
        return pl.ds(pl.multiple_of(index * size, size), size)

    rows_t = rows(x, T)
    rows_1 = rows(dp, R1)

    def copy(src, dst, ssem, rsem, zd, xd, bd):
        return pltpu.make_async_remote_copy(
            src_ref=src, dst_ref=dst, send_sem=ssem, recv_sem=rsem,
            device_id=(zd * X + xd, bd), device_id_type=MESH,
        )

    sent = []

    def send(*args):
        c = copy(*args)
        c.start()
        sent.append(c.wait_send)
        return c

    def send_if(cond, make):
        @pl.when(cond)
        def _():
            make().start()

        def done():
            @pl.when(cond)
            def _():
                make().wait_send()

        sent.append(done)

    WI = (wi, RX, wi_us, wi_ur, wi_ds, wi_dr)
    WO = (wo, R2, wo_us, wo_ur, wo_ds, wo_dr)

    def block(array, k, zz):
        return array[0].at[k, rows(zz, array[1]), :]

    def up(array, k, s):
        _, _, us, ur, _, _ = array
        send_if(
            jnp.logical_and(z >= s, z < Z - 1),
            lambda: copy(block(array, k, z - s), block(array, k, z - s), us.at[s, k], ur.at[s, k], z + 1, x, b),
        )

    def down(array, k, s):
        _, _, _, _, ds, dr = array
        send_if(
            jnp.logical_and(z + s < Z, z > 0),
            lambda: copy(block(array, k, z + s), block(array, k, z + s), ds.at[s, k], dr.at[s, k], z - 1, x, b),
        )

    def from_below(array, k, s):
        _, _, us, ur, _, _ = array

        @pl.when(z >= s + 1)
        def _():
            here = block(array, k, z - 1 - s)
            copy(here, here, us.at[s, k], ur.at[s, k], z - 1, x, b).wait_recv()

    def from_above(array, k, s):
        _, _, _, _, ds, dr = array

        @pl.when(z + 1 + s < Z)
        def _():
            here = block(array, k, z + 1 + s)
            copy(here, here, ds.at[s, k], dr.at[s, k], z + 1, x, b).wait_recv()

    def gather_start(array, k):
        up(array, k, 0)
        down(array, k, 0)

    def gather_pass(array, k):
        for s in range(Z - 2):
            from_below(array, k, s)
            up(array, k, s + 1)
            from_above(array, k, s)
            down(array, k, s + 1)

    def gather_end(array, k):
        from_below(array, k, Z - 2)
        from_above(array, k, Z - 2)

    GI = (gi_part, RX, gi_up, gi_dn, gi_us, gi_ur, gi_ds, gi_dr)
    GO = (go_part, R2, go_up, go_dn, go_us, go_ur, go_ds, go_dr)

    def add(array, k, d, here):
        part, size = array[0], array[1]
        r = pl.ds(d * size, size)
        part[k, r, :] = (part[k, r, :].astype(F32) + here[...].astype(F32)).astype(BF16)

    def sum_pass(array, k):
        part, size, ub, db, us, ur, ds, dr = array
        for i in range(Z - 1):
            d = Z - 1 - i

            def make_up(d=d):
                return copy(
                    part.at[k, pl.ds(d * size, size), :], ub.at[d, k], us.at[d, k], ur.at[d, k], z + 1, x, b
                )

            @pl.when(jnp.logical_and(z < d, z > 0))
            def _():
                make_up().wait_recv()
                add(array, k, d, ub.at[d, k])

            send_if(z < d, make_up)
            d = i

            def make_down(d=d):
                return copy(
                    part.at[k, pl.ds(d * size, size), :], db.at[d, k], ds.at[d, k], dr.at[d, k], z - 1, x, b
                )

            @pl.when(jnp.logical_and(z > d, z < Z - 1))
            def _():
                make_down().wait_recv()
                add(array, k, d, db.at[d, k])

            send_if(z > d, make_down)

    def sum_end(array, k, total):
        part, size, ub, db, us, ur, ds, dr = array
        mine = part.at[k, rows(z, size), :]
        total[...] = mine[...].astype(F32)

        @pl.when(z > 0)
        def _():
            copy(mine, ub.at[z, k], us.at[z, k], ur.at[z, k], z - 1, x, b).wait_recv()
            total[...] += ub[z, k].astype(F32)

        @pl.when(z < Z - 1)
        def _():
            copy(mine, db.at[z, k], ds.at[z, k], dr.at[z, k], z + 1, x, b).wait_recv()
            total[...] += db[z, k].astype(F32)

    barrier = pltpu.get_barrier_semaphore()

    def greet(zd, xd, bd):
        pl.semaphore_signal(barrier, inc=1, device_id=(zd * X + xd, bd), device_id_type=MESH)

    pl.when(z > 0)(lambda: greet(z - 1, x, b))
    pl.when(z < Z - 1)(lambda: greet(z + 1, x, b))
    for o in range(1, X):
        greet(z, xat(o), b)
    for k in range(1, L):
        greet(z, x, flip(k))
    wi[:, rows_1, :] = wi_ref[x]
    wo[:, rows(z, R2), :] = wo_ref[...]
    xg[0, rows_t, :] = x_ref[...]
    cg[rows_t, :] = ct_ref[...]
    inside = jnp.logical_and(z > 0, z < Z - 1)
    peers = X - 1 + L - 1
    pl.when(inside)(lambda: pl.semaphore_wait(barrier, peers + 2))
    pl.when(jnp.logical_not(inside))(lambda: pl.semaphore_wait(barrier, peers + 1))

    wx_c = [
        [
            send(wi_ref.at[xat(o), k], wi.at[k, rows_1, :], wx_s.at[o, k], wx_r.at[o, k], z, xat(o), b)
            for o in range(1, X)
        ]
        for k in range(L)
    ]
    xx_c = [send(x_ref, xg.at[0, rows_t, :], xx_s.at[o], xx_r.at[o], z, xat(o), b) for o in range(1, X)]
    x_c = [
        send(x_ref, xg.at[k, rows_t, :], x_s.at[k, 0], x_r.at[k, 0], z, x, flip(k))
        for k in reversed(range(1, L))
    ]
    for k in range(L):
        for c in wx_c[k]:
            c.wait_recv()
        gather_start(WI, k)
    for o in range(1, X):
        xx_c[o - 1].wait_recv()
        theirs = rows((x + X - o) % X, T)
        for k in reversed(range(1, L)):
            x_c.append(
                send(xg.at[0, theirs, :], xg.at[k, theirs, :], x_s.at[k, o], x_r.at[k, o], z, x, flip(k))
            )
    ct_c = [send(ct_ref, cg.at[rows_t, :], ct_s.at[o], ct_r.at[o], z, xat(o), b) for o in range(1, X)]
    for k in range(L):
        gather_pass(WI, k)
    back_order = list(reversed(range(L)))
    for k in back_order:
        gather_start(WO, k)
    for c in x_c:
        c.wait_recv()
    for k in range(L):
        gather_end(WI, k)

    def activate(r):
        v = dot(xg[0, r, :], wi[0], 1, 0)
        for k in range(1, L):
            v = v + dot(xg[k, r, :], wi[k], 1, 0)
        pa[r, :] = v
        t = jnp.tanh(GELU_C * v * (1.0 + GELU_A * (v * v)))
        hg[0, r, :] = (v * (0.5 + 0.5 * t)).astype(BF16)

    tiles(TX, 128, activate)
    hg_c = [
        send(hg.at[0], hg.at[k], hg_s.at[k], hg_r.at[k], z, x, flip(k))
        for k in reversed(range(1, L))
    ]
    gather_pass(WO, back_order[0])
    for c in ct_c:
        c.wait_recv()

    def grad_out(k):
        def one(r):
            go_part[k, r, :] = dot(hg[k, :, r], cg[...], 0, 0).astype(BF16)

        if k:
            hg_c[L - 1 - k].wait_recv()
        tiles(HX, 256, one)

    def hid_term(k):
        def one(r):
            term = dot(cg[r, :], wo[k], 1, 1).astype(BF16)
            if k:
                ht_send[k - 1, r, :] = term
            else:
                ht_own[r, :] = term

        gather_end(WO, k)
        tiles(TX, 256, one)
        if k:
            ht_c.append(send(ht_send.at[k - 1], ht_recv.at[k - 1], ht_s.at[k], ht_r.at[k], z, x, flip(k)))

    ht_c = []
    grad_out(0)
    for j, k in enumerate(back_order):
        if j + 1 < L:
            gather_pass(WO, back_order[j + 1])
        hid_term(k)
        if j + 1 < L:
            sum_pass(GO, j)
            grad_out(j + 1)

    for c in ht_c:
        c.wait_recv()

    def slope(r):
        g = ht_own[r, :].astype(F32)
        for k in range(1, L):
            g = g + ht_recv[k - 1, r, :].astype(F32)
        v = pa[r, :]
        v2 = v * v
        t = jnp.tanh(GELU_C * v * (1.0 + GELU_A * v2))
        d = 0.5 + 0.5 * t + 0.5 * v * (1.0 - t * t) * (GELU_C * (1.0 + 3.0 * GELU_A * v2))
        pg[r, :] = (g * d).astype(BF16)

    sum_pass(GO, L - 1)
    tiles(TX, 128, slope)

    def grad_in(k):
        def one(r):
            gi_part[k, r, :] = dot(xg[k, :, r], pg[...], 0, 0).astype(BF16)

        tiles(C, 256, one)

    ig_c = []

    def grad_x(k):
        def one(r):
            ig_send[k, r, :] = dot(pg[r, :], wi[k], 1, 1).astype(BF16)

        tiles(TX, 256, one)
        if k:
            ig_c.append(send(ig_send.at[k], ig_recv.at[k - 1], ig_s.at[k], ig_r.at[k], z, x, flip(k)))

    grad_in(0)
    for j, k in enumerate(back_order):
        grad_x(k)
        if j + 1 < L:
            grad_in(j + 1)
        if j == 0:
            def forward(r):
                total = dot(hg[0, r, :], wo[0], 1, 0)
                for i in range(1, L):
                    total = total + dot(hg[i, r, :], wo[i], 1, 0)
                o_send[r, :] = total.astype(BF16)

        sum_pass(GI, j)
    tiles(TX, 256, forward)
    o_c = [
        send(o_send.at[rows(xat(o), T), :], o_recv.at[o], o_s.at[o], o_r.at[o], z, xat(o), b)
        for o in range(1, X)
    ]
    for c in ig_c:
        c.wait_recv()

    def add_terms(r):
        total = ig_send[0, r, :].astype(F32)
        for k in range(1, L):
            total = total + ig_recv[k - 1, r, :].astype(F32)
        ig_sum[r, :] = total.astype(BF16)

    tiles(TX, 128, add_terms)
    igx_c = [
        send(ig_sum.at[rows(xat(o), T), :], ig_x.at[o], igx_s.at[o], igx_r.at[o], z, xat(o), b)
        for o in range(1, X)
    ]
    for k in range(L):
        sum_end(GO, k, go_ref.at[k])

    gx_c = []
    for k in range(L):
        sum_end(GI, k, acc)
        gx_send[k] = acc[...].astype(BF16)
        gi_ref[x, k] = acc[rows(x, R1), :]
        for o in range(1, X):
            gx_c.append(
                send(gx_send.at[k, rows(xat(o), R1), :], gx_recv.at[o, k], gx_s.at[o, k], gx_r.at[o, k], z, xat(o), b)
            )
    for mine, theirs, copies, result in ((o_send, o_recv, o_c, out_ref), (ig_sum, ig_x, igx_c, ig_ref)):
        total = mine[rows_t, :].astype(F32)
        for o in range(1, X):
            copies[o - 1].wait_recv()
            total = total + theirs[o].astype(F32)
        result[...] = total.astype(BF16)
    for c in gx_c:
        c.wait_recv()
    for o in range(1, X):
        gi_ref[(x + X - o) % X] = gx_recv[o].astype(F32)
    for done in sent:
        done()


def body(Z, X, inputs, weight_in, weight_out, cotangent):
    T, C = inputs.shape
    R1, L, panel = weight_in.shape
    R2 = weight_out.shape[0]
    TX, HX, RX = X * T, Z * R2, X * R1
    wi = weight_in.reshape(R1, L, Z, X, R2).transpose(3, 1, 0, 2, 4).reshape(X, L, R1, HX)
    wo = weight_out.transpose(1, 0, 2)
    vmem = pl.BlockSpec(memory_space=pltpu.VMEM)

    def buf(*shape):
        return pltpu.VMEM(shape, BF16)

    def sems(*shape):
        return [pltpu.SemaphoreType.DMA(shape)] * 2

    flops = 12 * TX * HX * C * L
    out, ig, gi, go = pl.pallas_call(
        functools.partial(kernel, Z, X, L),
        out_shape=(
            jax.ShapeDtypeStruct((T, C), BF16),
            jax.ShapeDtypeStruct((T, C), BF16),
            jax.ShapeDtypeStruct((X, L, R1, HX), F32),
            jax.ShapeDtypeStruct((L, R2, C), F32),
        ),
        in_specs=[vmem] * 4,
        out_specs=(vmem,) * 4,
        scratch_shapes=[
            buf(L, HX, C), buf(L, C, HX), buf(L, TX, C), buf(TX, C), pltpu.VMEM((TX, HX), F32),
            buf(TX, HX), buf(L - 1, TX, HX), buf(L - 1, TX, HX), buf(L, TX, HX), buf(TX, HX),
            buf(L, C, HX), buf(Z, L, RX, HX), buf(Z, L, RX, HX), buf(L, RX, HX), buf(X, L, R1, HX),
            pltpu.VMEM((RX, HX), F32),
            buf(L, HX, C), buf(Z, L, R2, C), buf(Z, L, R2, C),
            buf(L, TX, C), buf(L - 1, TX, C), buf(TX, C), buf(X, T, C), buf(TX, C), buf(X, T, C),
            *sems(Z - 1, L), *sems(Z - 1, L), *sems(Z - 1, L), *sems(Z - 1, L),
            *sems(Z, L), *sems(Z, L), *sems(Z, L), *sems(Z, L),
            *sems(X, L), *sems(X, L), *sems(X), *sems(L, X), *sems(X), *sems(L), *sems(L), *sems(L),
            *sems(X), *sems(X),
        ],
        compiler_params=pltpu.CompilerParams(
            collective_id=0, has_side_effects=True, vmem_limit_bytes=60 * 2**20
        ),
        cost_estimate=pl.CostEstimate(flops=flops, bytes_accessed=8 * 2**20, transcendentals=TX * HX),
    )(inputs, cotangent, wi, wo)
    grad_in = gi.reshape(X, L, R1, Z, R2).transpose(2, 1, 3, 0, 4).reshape(R1, L, panel)
    return out, ig, grad_in, go.transpose(1, 0, 2)


def solution(mesh):
    n = mesh.shape["dp"]
    Z = 4 if n % 4 == 0 else n
    placed = (P("dp", "block"), P("dp", None, "block"), P("dp", None, "block"), P("dp", "block"))
    return jax.shard_map(
        functools.partial(body, Z, n // Z),
        mesh=mesh,
        in_specs=placed,
        out_specs=(
            P("dp", "block"),
            P("dp", "block"),
            P("dp", None, "block"),
            P("dp", None, "block"),
        ),
        check_vma=False,
    )
```

time: 392 us -> 162 us (0.41)
  waiting for transfers between devices: 330 us -> 0 us
  Pallas kernels: 0 us -> 153 us
  matrix products: 22.1 us -> 0 us
  between operations: 14.6 us -> 0.68 us
  starting transfers between devices: 5.58 us -> 0 us
  local copies, waits for them, and re-layouts: 13.3 us -> 8.15 us
  other arithmetic: 4.03 us -> 0 us
    pallas_call x0 -> x1, Pallas kernels: none -> 153 us  [body(): pl.pallas_call(functools.partial(kernel, Z, X, L), out_shape=(jax.ShapeDt...]
    unnamed x5 -> x0, waiting for transfers between devices: 108 us -> none
    all_gather x2 -> x0, waiting for transfers between devices: 92.4 us -> none  [the longest x1 63.1 us: body(): lax.all_gather(weight_out, 'dp', axis=0, tiled=True)]
    reduce_scatter x1 -> x0, waiting for transfers between devices: 76.3 us -> none  [reduce_out(): lax.psum_scatter(term(jnp.int32(0), lax.axis_size('dp') * shard_rows).ast...]
    ppermute x8 -> x0, waiting for transfers between devices: 52.7 us -> none  [swapped(): return lax.ppermute(value, axis, pairs)]
    dot_general x6 -> x0, matrix products: 22.1 us -> none  [the longest x1 5.9 us: body(): jnp.einsum('tkc,ckh->th', in_stack, weight_in_all, preferred_element_type...]
    convert_element_type x3 -> x0, local copies, waits for them, and re-layouts: 5.95 us -> none  [the longest x1 5.66 us: reduce_in(): term(jnp.int32(0), lax.axis_size('dp') * shard_rows).astype(jnp.bfloat16)]
    ppermute x8 -> x0, starting transfers between devices: 5.43 us -> none  [swapped(): return lax.ppermute(value, axis, pairs)]
  transfers between devices with their start and end apart: 12 -> 0, of which waited for: 9 -> 0; matrix products, arithmetic and copies ran while one was open for 5% -> 0% of each run, Pallas kernels for 0% -> 0%
where the time goes in v2:
time: 162 us; the launch traced here: 161 us
  Pallas kernels  153 us (94%)
  local copies, waits for them, and re-layouts  8.15 us (5%)
    pallas_call x1, Pallas kernels, body(): pl.pallas_call(functools.partial(kernel, Z, X, L), out_shape=(jax.ShapeDt...  153 us

profile of v2, /device:TPU:8, one launch (start us, length us, event | category | flops | bytes accessed | tf_op | source)
XLA Modules:
  0.0 161.4 jit_solution(12535033372168096138)
XLA Ops:
  0.6 1.3 reshape.20
  1.9 0.1 copy.11
  2.0 0.9 reshape.21.wi_ref
  2.9 152.6 %shard_map.75 = (bf16[384,512]{1,0:T(8,128)(2,1)}, bf16[384,512]{1,0:T(8,128)(2,1)}, f32[2,3,64,512]{3,2,1,0:T(8,128)}, f32[3,128,512]{2,1,0:T(8,128)}) custom-call(bf16[384,512]{1,0:T(8,128)(2,1)} %x_ref.1, bf16[384,512]{1,0:T(8,128)(2,1)} %ct_ref.1, bf16[2,3,64,512]{3,2,1,0:T(8,128)(2,1)} %reshape.21.wi_ref, bf16[3,128,512]{2,1,0:T(8,128)(2,1)} %bitcast.15), custom_call_target="tpu_custom_call" | custom-call | flops 7247757312 | bytes 8388608 | tf_op jit(solution)/shard_map/pallas_call | solution.py:393
  155.5 1.4 reshape.22
  156.9 0.6 copy.9
  157.5 0.0 copy-start.2
  157.5 0.0 copy-start.1
  157.5 1.5 reshape.23
  159.0 0.0 copy-done.2
  159.0 0.0 copy-start
  159.1 0.7 copy.15
  159.8 0.0 copy-done.1
  159.8 0.7 copy.16
  160.5 0.0 copy-done
  160.5 0.9 copy.17
Async XLA Ops:
  157.5 1.5 copy-start.2
  157.5 2.3 %copy-start.1 = (bf16[384,512]{1,0:T(8,128)(2,1)S(1)}, bf16[384,512]{1,0:T(8,128)(2,1)}, u32[]{:S(2)}) copy-start(bf16[384,512]{1,0:T(8,128)(2,1)} %get-tuple-element.17) | copy-start | bytes 1179652
  159.0 1.5 copy-start

commit v3 on v2

--- a/solution.py
+++ b/solution.py
@@ -137,35 +137,47 @@
         r = pl.ds(d * size, size)
         part[k, r, :] = (part[k, r, :].astype(F32) + here[...].astype(F32)).astype(BF16)
 
-    def sum_pass(array, k):
-        part, size, ub, db, us, ur, ds, dr = array
-        for i in range(Z - 1):
-            d = Z - 1 - i
-
-            def make_up(d=d):
+    low = z < Z // 2
+
+    def sum_up(array, k, half):
+        part, size, ub, _, us, ur, _, _ = array
+        for d in reversed(range(1, Z)):
+
+            def make(d=d):
                 return copy(
                     part.at[k, pl.ds(d * size, size), :], ub.at[d, k], us.at[d, k], ur.at[d, k], z + 1, x, b
                 )
 
-            @pl.when(jnp.logical_and(z < d, z > 0))
+            @pl.when(jnp.logical_and(half, jnp.logical_and(z < d, z > 0)))
             def _():
-                make_up().wait_recv()
+                make().wait_recv()
                 add(array, k, d, ub.at[d, k])
 
-            send_if(z < d, make_up)
-            d = i
-
-            def make_down(d=d):
+            send_if(jnp.logical_and(half, z < d), make)
+
+    def sum_down(array, k, half):
+        part, size, _, db, _, _, ds, dr = array
+        for d in range(Z - 1):
+
+            def make(d=d):
                 return copy(
                     part.at[k, pl.ds(d * size, size), :], db.at[d, k], ds.at[d, k], dr.at[d, k], z - 1, x, b
                 )
 
-            @pl.when(jnp.logical_and(z > d, z < Z - 1))
+            @pl.when(jnp.logical_and(half, jnp.logical_and(z > d, z < Z - 1)))
             def _():
-                make_down().wait_recv()
+                make().wait_recv()
                 add(array, k, d, db.at[d, k])
 
-            send_if(z > d, make_down)
+            send_if(jnp.logical_and(half, z > d), make)
+
+    def sum_near(array, k):
+        sum_up(array, k, low)
+        sum_down(array, k, jnp.logical_not(low))
+
+    def sum_far(array, k):
+        sum_down(array, k, low)
+        sum_up(array, k, jnp.logical_not(low))
 
     def sum_end(array, k, total):
         part, size, ub, db, us, ur, ds, dr = array
@@ -281,9 +293,13 @@
             gather_pass(WO, back_order[j + 1])
         hid_term(k)
         if j + 1 < L:
-            sum_pass(GO, j)
+            sum_near(GO, j)
             grad_out(j + 1)
-
+        if j and j + 1 < L:
+            sum_far(GO, j - 1)
+
+    sum_near(GO, L - 1)
+    sum_far(GO, L - 2)
     for c in ht_c:
         c.wait_recv()
 
@@ -297,7 +313,6 @@
         d = 0.5 + 0.5 * t + 0.5 * v * (1.0 - t * t) * (GELU_C * (1.0 + 3.0 * GELU_A * v2))
         pg[r, :] = (g * d).astype(BF16)
 
-    sum_pass(GO, L - 1)
     tiles(TX, 128, slope)
 
     def grad_in(k):
@@ -317,10 +332,13 @@
             ig_c.append(send(ig_send.at[k], ig_recv.at[k - 1], ig_s.at[k], ig_r.at[k], z, x, flip(k)))
 
     grad_in(0)
+    sum_near(GI, 0)
+    sum_far(GO, L - 1)
     for j, k in enumerate(back_order):
         grad_x(k)
         if j + 1 < L:
             grad_in(j + 1)
+            sum_near(GI, j + 1)
         if j == 0:
             def forward(r):
                 total = dot(hg[0, r, :], wo[0], 1, 0)
@@ -328,7 +346,7 @@
                     total = total + dot(hg[i, r, :], wo[i], 1, 0)
                 o_send[r, :] = total.astype(BF16)
 
-        sum_pass(GI, j)
+        sum_far(GI, j)
     tiles(TX, 256, forward)
     o_c = [
         send(o_send.at[rows(xat(o), T), :], o_recv.at[o], o_s.at[o], o_r.at[o], z, xat(o), b)

time: 162 us -> 136 us (0.84)
  Pallas kernels: 153 us -> 127 us
    pallas_call x1, Pallas kernels: 153 us -> 127 us  [body(): pl.pallas_call(functools.partial(kernel, Z, X, L), out_shape=(jax.ShapeDt...]
where the time goes in v3:
time: 136 us; the launch traced here: 135 us
  Pallas kernels  127 us (93%)
  local copies, waits for them, and re-layouts  8.15 us (6%)
    pallas_call x1, Pallas kernels, body(): pl.pallas_call(functools.partial(kernel, Z, X, L), out_shape=(jax.ShapeDt...  127 us
    reshape x2, local copies, waits for them, and re-layouts, body(): gi.reshape(X, L, R1, Z, R2).transpose(2, 1, 3, 0, 4).reshape(R1, L, panel)  2.9 us

profile of v3, /device:TPU:8, one launch (start us, length us, event | category | flops | bytes accessed | tf_op | source)
XLA Modules:
  0.0 135.4 jit_solution(100243077906937640)
XLA Ops:
  0.6 1.3 reshape.20
  1.9 0.1 copy.11
  2.0 0.9 reshape.21.wi_ref
  2.9 126.6 %shard_map.75 = (bf16[384,512]{1,0:T(8,128)(2,1)}, bf16[384,512]{1,0:T(8,128)(2,1)}, f32[2,3,64,512]{3,2,1,0:T(8,128)}, f32[3,128,512]{2,1,0:T(8,128)}) custom-call(bf16[384,512]{1,0:T(8,128)(2,1)} %x_ref.1, bf16[384,512]{1,0:T(8,128)(2,1)} %ct_ref.1, bf16[2,3,64,512]{3,2,1,0:T(8,128)(2,1)} %reshape.21.wi_ref, bf16[3,128,512]{2,1,0:T(8,128)(2,1)} %bitcast.15), custom_call_target="tpu_custom_call" | custom-call | flops 7247757312 | bytes 8388608 | tf_op jit(solution)/shard_map/pallas_call | solution.py:411
  129.5 1.4 %reshape.22 = f32[2,3,64,4,128]{4,3,2,1,0:T(4,128)S(1)} reshape(f32[2,3,64,512]{3,2,1,0:T(8,128)} %get-tuple-element.10) | data formatting | bytes 1572864 | tf_op jit(solution)/shard_map/reshape | solution.py:438
  130.9 0.6 copy.9
  131.5 0.0 copy-start.2
  131.5 0.0 copy-start.1
  131.5 1.5 %reshape.23 = f32[64,3,1024]{2,0,1:T(8,128)} reshape(f32[64,3,4,2,128]{4,3,2,0,1:T(2,128)S(1)} %copy.9) | data formatting | bytes 1572864 | tf_op jit(solution)/shard_map/reshape | solution.py:438
  133.0 0.0 copy-done.2
  133.0 0.0 copy-start
  133.0 0.7 copy.15
  133.8 0.0 copy-done.1
  133.8 0.7 copy.16
  134.5 0.0 copy-done
  134.5 0.9 copy.17
Async XLA Ops:
  131.5 1.5 %copy-start.2 = (bf16[384,512]{1,0:T(8,128)(2,1)S(1)}, bf16[384,512]{1,0:T(8,128)(2,1)}, u32[]{:S(2)}) copy-start(bf16[384,512]{1,0:T(8,128)(2,1)} %get-tuple-element.16) | copy-start | bytes 1179652
  131.5 2.3 %copy-start.1 = (bf16[384,512]{1,0:T(8,128)(2,1)S(1)}, bf16[384,512]{1,0:T(8,128)(2,1)}, u32[]{:S(2)}) copy-start(bf16[384,512]{1,0:T(8,128)(2,1)} %get-tuple-element.17) | copy-start | bytes 1179652
  133.0 1.5 %copy-start = (f32[3,128,512]{2,1,0:T(8,128)S(1)}, f32[3,128,512]{2,1,0:T(8,128)}, u32[]{:S(2)}) copy-start(f32[3,128,512]{2,1,0:T(8,128)} %get-tuple-element.11) | copy-start | bytes 2359300
